TPU v7x, 128 devices: a whole 4x4x4 slice. The times are simulated.
128 devices in a mesh: grp: 8 (over x, core), blk: 16 (over y, z).
Axes of the slice: x: 4, y: 4, z: 4, core: 2. Of those that a mesh axis runs over, the one named last changes fastest.
Arguments:
- flow_state: float32 [5, 1024, 4096], P(None, 'grp', 'blk'), may hold values from -6 to 6
- jacobi_x: float32 [5, 5], replicated, may hold values from -2.5 to 2.5
- jacobi_y: float32 [5, 5], replicated, may hold values from -2.5 to 2.5
- slot_tile: int32 [8192], P(('grp', 'blk')), may hold values from -1 to 95, as said below
- slot_cells: int32 [8192, 128], P(('grp', 'blk')), may hold values from 0 to 32767
- slot_normal: float32 [8192, 3, 128], P(('grp', 'blk')), may hold values from -6 to 6
- slot_rbf: bfloat16 [8192, 128, 128], P(('grp', 'blk')), may hold values from -0.5 to 0.5
- disp_in: float32 [1536, 3, 128], P('blk'), may hold values from -24 to 24
- flexibility: float32 [1536, 128, 128], P('blk'), may hold values from -0.5 to 0.5
- secant_v: float32 [24, 1536, 3, 128], P(None, 'blk'), may hold values from -3.4 to 3.4
- secant_w: float32 [24, 1536, 3, 128], P(None, 'blk'), may hold values from -6 to 6
Outputs:
- flow_out: float32 [5, 1024, 4096], P(None, 'grp', 'blk')
- disp_out: float32 [1536, 3, 128], P('blk')
Inputs may be any that keep to these rules, and one draw needn't show every extreme that they name: `slot_tile`: each fluid block has at most 4 live slots for each structure partition, its live slots to a partition come first among that partition's 4 slots, and every fluid block fills all 4 slots of one partition.
All inputs are finite; a program needn't handle non-finite values.
Results may differ from a plain program's by a relative error of at most 0.002.
Values may be sent and summed in bfloat16 or wider, within the bound.
A program may use at most 128 MiB of HBM per device.

v0:
```python
import functools

import jax
import jax.numpy as jnp
from jax import lax
from jax.experimental import pallas as pl
from jax.experimental.pallas import tpu as pltpu
from jax.sharding import PartitionSpec as P

RATES = (0.25, 1.0 / 3.0, 0.5, 1.0)
TIME_STEP = 0.4
DAMPING = 0.25
FORCING = 1.0
F32 = jnp.float32
BF16 = jnp.bfloat16
F8 = jnp.float8_e4m3fn
LIFT = 64.0
MESH = pl.DeviceIdType.MESH
NG, NB = 8, 16
SEND, ST, COLS, NV = 4, 96, 24, 5
CX, CY = 128, 256
OWN = ST // NG
WIN = 16
HOPS = ((0, 0), (0, 1), (0, 3), (1, 0), (3, 0), (2, 2), (1, 1), (1, 3), (3, 1), (3, 3), (0, 2), (2, 0), (1, 2), (3, 2), (2, 1), (2, 3))
BACK = tuple(HOPS.index(((4 - dy) % 4, (4 - dz) % 4)) for dy, dz in HOPS)
ME = HOPS.index((0, 0))
CLASSES = ((1, 5), (6, 12), (12, 16))
FAR = 5
NN = (((1,), (0,)), ((), ()))
NT = (((1,), (1,)), ((), ()))


def iota(shape, dim):
    return lax.broadcasted_iota(jnp.int32, shape, dim)


def dot(a, b, dims):
    return lax.dot_general(a, b, dims, preferred_element_type=F32)


def split(x):
    hi = x.astype(BF16)
    return hi, (x - hi.astype(F32)).astype(BF16)


def window(g):
    return lax.div(g * OWN, 8) * 8


def kernel(
    flow_h, jx_h, jy_h, tile_h, cells_h, normal_h, rbf_h, disp_h, flex_h, secv_h, secw_h,
    flow_o, disp_o,
    jx, jy, tile, cells, normal, rbf, disp, flex, secv, secw,
    force_q, qa, qb, qout, rows0, rows1, rows2,
    req, land_req, resp, land_disp, dispc, cellv, rall, rall8, bmat, bmat8, acc, table, pack,
    land_below, land_above, land_right, land_left, land_corner,
    nrm, norms, load_out, land_load, oht, part, land_part,
    flexhl, uwin, zmat, gsend, land_gg, gsum, land_gb, linv,
    rmsg, land_rg, tmsg, land_t, rsend, land_r, coef, dout,
    lsem, rsem, osem, bs, br, gs, gr, hs, hr,
):
    g = lax.axis_index("grp")
    b = lax.axis_index("blk")
    y, z = lax.div(b, 4), lax.rem(b, 4)
    a = pl.multiple_of(window(g), 8)
    off = g * OWN - window(g)

    def peer(o):
        return lax.rem(y + HOPS[o][0], 4) * 4 + lax.rem(z + HOPS[o][1], 4)

    loads = [
        (tile_h, tile),
        (cells_h, cells),
        (disp_h, disp),
        (secv_h.at[:, :, pl.ds(a, WIN), :], secv),
        (flow_h, force_q.at[:, pl.ds(8, CX), pl.ds(0, CY)]),
        (normal_h, normal),
        (flex_h.at[pl.ds(a, WIN)], flex),
        (jx_h, jx),
        (jy_h, jy),
        (secw_h, secw),
    ]
    loads = [pltpu.make_async_copy(s, d, lsem.at[i]) for i, (s, d) in enumerate(loads)]
    l_tile, l_cells, l_disp, l_secv, l_flow, l_normal, l_flex, l_jx, l_jy, l_secw = loads
    l_rbf = [
        pltpu.make_async_copy(rbf_h.at[pl.ds(peer(o) * SEND, SEND)], rbf.at[o], rsem.at[o]) for o in range(NB)
    ]
    l_tile.start()

    barrier = pltpu.get_barrier_semaphore()
    g_up, g_dn = lax.rem(g + 1, NG), lax.rem(g + NG - 1, NG)
    b_up, b_dn = lax.rem(b + 1, NB), lax.rem(b + NB - 1, NB)
    hello = [(g, peer(o)) for o in reversed(range(NB)) if o != ME]
    hello += [(g_dn, b_dn), (g_dn, b_up), (g_up, b_dn), (g_up, b_up)]
    hello += [(lax.rem(g + o, NG), b) for o in range(1, NG)]
    for dev in hello:
        pl.semaphore_signal(barrier, inc=1, device_id=dev, device_id_type=MESH)

    for c in loads[1:4] + l_rbf + loads[4:]:
        c.start()

    def blk_copy(src, land, ph, o):
        return pltpu.make_async_remote_copy(
            src_ref=src(o), dst_ref=land.at[BACK[o]], send_sem=bs.at[ph, o], recv_sem=br.at[ph, BACK[o]],
            device_id=(g, peer(o)), device_id_type=MESH,
        )

    def grp_copy(src, dst, ph, o, dev):
        return pltpu.make_async_remote_copy(
            src_ref=src, dst_ref=dst, send_sem=gs.at[ph, o], recv_sem=gr.at[ph, o],
            device_id=(dev, b), device_id_type=MESH,
        )

    def each(n, step):
        def body(o, _):
            step(o)
            return 0

        lax.fori_loop(1, n, body, 0)

    pending = []

    def finish():
        for wait in pending:
            wait()

    far_first = [FAR] + [o for o in reversed(range(NB)) if o not in (ME, FAR)]

    def blk_send(src, land, ph, peers=far_first):
        for o in peers:
            copy = blk_copy(src, land, ph, o)
            copy.start()
            pending.append(copy.wait_send)

    def blk_recv(src, land, ph, peers=far_first[::-1]):
        for o in peers:
            pltpu.make_async_remote_copy(
                src_ref=src(o), dst_ref=land.at[o], send_sem=bs.at[ph, o], recv_sem=br.at[ph, o],
                device_id=(g, peer(o)), device_id_type=MESH,
            ).wait_recv()

    def grp_send(src, land, ph):
        def step(o):
            d = lax.rem(g + o, NG)
            grp_copy(src(d), land.at[g], ph, o, d).start()

        def last(o):
            grp_copy(src(0), land.at[0], ph, o, 0).wait_send()

        each(NG, step)
        pending.append(lambda: each(NG, last))

    def grp_recv(src, land, ph):
        def step(o):
            d = lax.rem(g + NG - o, NG)
            grp_copy(src(d), land.at[d], ph, o, d).wait_recv()

        each(NG, step)

    l_tile.wait()
    row = iota((NB * 16, 64), 0)
    hit = iota((NB * 16, 64), 1) == lax.shift_right_logical(row, 4) * SEND + (row & 3)
    wanted = jnp.sum(jnp.where(hit, tile[...].astype(F32), 0.0), axis=1, keepdims=True)
    row = iota((NB * 16, 128), 0)
    wanted = jnp.where((row & 15) < 12, jnp.broadcast_to(wanted, (NB * 16, 128)), -1.0)
    req[...] = wanted.reshape(NB, 16, 128)
    land_req[ME] = req[b]

    pl.semaphore_wait(barrier, len(hello))
    blk_send(lambda o: req.at[peer(o)], land_req, 0)

    l_disp.wait()
    dispc[...] = jnp.zeros(dispc.shape, BF16)
    for c in range(3):
        dispc[128 * c : 128 * c + ST, :] = disp[c].astype(BF16)
    to_far = pltpu.make_async_remote_copy(
        src_ref=dispc, dst_ref=table, send_sem=osem.at[2], recv_sem=osem.at[3],
        device_id=(g, peer(FAR)), device_id_type=MESH,
    )
    to_far.start()
    pending.append(to_far.wait_send)

    l_cells.wait()
    for o in range(NB):
        cellv[o, 0:SEND, :] = cells[pl.ds(peer(o) * SEND, SEND), :]

    def rows_of(p, _):
        for i in range(4):
            for j in range(SEND):
                cell = cellv[4 * p + i, j : j + 1, :]
                r = (lax.shift_right_logical(cell, 7) & 1) * 128 + lax.shift_right_logical(cell, 8)
                one = jnp.where(iota((256, 128), 0) == r, 1.0, 0.0)
                rall[p, :, 512 * i + 128 * j : 512 * i + 128 * (j + 1)] = one.astype(BF16)
                rall8[p, :, 512 * i + 128 * j : 512 * i + 128 * (j + 1)] = one.astype(F8)
                cellv[4 * p + i, SEND + j : SEND + j + 1, :] = cell & 127
        return 0

    lax.fori_loop(0, 4, rows_of, 0)
    l_normal.wait()
    nrm[...] = jnp.zeros(nrm.shape, F32)
    for c in range(3):
        for j in range(SEND):
            nrm[pl.ds(4 * c + j, NB, stride=16), :] = normal[c, pl.ds(j, NB, stride=SEND), :]
    for o in range(NB):
        norms[o] = nrm[pl.ds(pl.multiple_of(peer(o) * 16, 16), 16), :]
    force_q[:, 0:8, :] = jnp.zeros((NV, 8, CY + 128), F32)
    force_q[:, 8 + CX : 16 + CX, :] = jnp.zeros((NV, 8, CY + 128), F32)
    force_q[:, 8 : 8 + CX, CY : CY + 128] = jnp.zeros((NV, CX, 128), F32)
    def answer(asked, shown):
        n = asked.shape[0] * 16
        asked = asked.reshape(n, 128)
        row_c = lax.shift_right_logical(iota((n, 128), 0), 2) & 3
        found = asked == iota((n, 128), 1).astype(F32)
        pick = jnp.concatenate([jnp.where(found & (row_c == c), 1.0, 0.0).astype(BF16) for c in range(3)], axis=1)
        return dot(pick, shown, NN).astype(BF16).reshape(n // 16, 16, 128)

    land_disp[ME] = answer(land_req[ME][None], dispc[...])[0]
    for first, last in CLASSES:
        blk_recv(lambda o: req.at[peer(o)], land_req, 0, range(first, last))
        resp[first:last] = answer(land_req[first:last], dispc[...])
        blk_send(lambda o: resp.at[o], land_disp, 1, range(first, last))

    acc[...] = jnp.zeros(acc.shape, F32)
    none16 = jnp.zeros((16, 128), BF16)

    def spread(p, _):
        @pl.when(p == FAR // 4)
        def _():
            to_far.wait_recv()
            land_disp[FAR] = answer(req[peer(FAR)][None], table[...])[0]

        for i in range(4):
            o = 4 * p + i

            @pl.when((o != ME) & (o != FAR))
            def _():
                pltpu.make_async_remote_copy(
                    src_ref=resp.at[o], dst_ref=land_disp.at[o], send_sem=bs.at[1, o], recv_sem=br.at[1, o],
                    device_id=(g, peer(FAR)), device_id_type=MESH,
                ).wait_recv()

            pltpu.make_async_copy(rbf_h.at[pl.ds(0, SEND)], rbf.at[o], rsem.at[o]).wait()
        for h in (0, 2):
            o = 4 * p + h
            x = jnp.concatenate(
                [
                    jnp.concatenate([land_disp[o], none16], axis=1),
                    jnp.concatenate([none16, land_disp[o + 1]], axis=1),
                ],
                axis=0,
            )
            weights = [rbf[o + i].reshape(SEND * 128, 128) for i in range(2)]
            moved = dot(x, jnp.concatenate(weights, axis=1), NT) * FORCING
            high = moved.astype(BF16).astype(F32)
            low = (moved - high) * LIFT
            for i in range(2):
                for j in range(SEND):
                    mask = iota((128, 128), 0) == cellv[o + i, SEND + j : SEND + j + 1, :]
                    at = 512 * (h + i) + 128 * j
                    for c in range(3):
                        r = 16 * i + 4 * c + j
                        vh = high[r : r + 1, 128 * j : 128 * (j + 1)]
                        vl = low[r : r + 1, 128 * j : 128 * (j + 1)]
                        bmat[128 * c : 128 * c + 128, at : at + 128] = jnp.where(mask, vh, 0.0).astype(BF16)
                        bmat8[128 * c : 128 * c + 128, at : at + 128] = jnp.where(mask, vl, 0.0).astype(F8)
        acc[...] += dot(bmat[...], rall[p], NT) + dot(bmat8[...], rall8[p], NT) * (1.0 / LIFT)
        return 0

    lax.fori_loop(0, 4, spread, 0)
    l_flow.wait()
    for c in range(3):
        s = acc[128 * c : 128 * c + 128, :]
        force_q[1 + c, 8 : 8 + CX, 0:128] += s[:, 0:128].T
        force_q[1 + c, 8 : 8 + CX, 128:256] += s[:, 128:256].T

    lane = iota((128, 128), 1)
    strip = lax.shift_right_logical((lane + 4) & 127, 3)
    packed = jnp.zeros((128, 128), F32)
    for v in range(NV):
        t = jnp.where(lane < 64, force_q[v, 8 : 8 + CX, 0:128], force_q[v, 8 : 8 + CX, 128:256])
        if v:
            t = pltpu.roll(t, 8 * v, 1)
        packed = jnp.where(strip == v, t, packed)
    lane64 = iota((64, 128), 1)
    pack[...] = jnp.where(((lane64 + 4) & 127) < 64, packed[0:64], pltpu.roll(packed[64:128], 64, 1))
    top_rows = force_q.at[:, pl.ds(8, 8), pl.ds(0, CY)]
    low_rows = force_q.at[:, pl.ds(CX, 8), pl.ds(0, CY)]
    halo = [
        (pack.at[pl.ds(0, 8)], land_corner.at[0], (g_dn, b_dn)),
        (pack.at[pl.ds(0, 8)], land_corner.at[1], (g_dn, b_up)),
        (pack.at[pl.ds(56, 8)], land_corner.at[2], (g_up, b_dn)),
        (pack.at[pl.ds(56, 8)], land_corner.at[3], (g_up, b_up)),
        (pack, land_right, (g, b_dn)),
        (pack, land_left, (g, b_up)),
        (top_rows, land_below, (g_dn, b)),
        (low_rows, land_above, (g_up, b)),
    ]
    halo = [
        pltpu.make_async_remote_copy(
            src_ref=s, dst_ref=d, send_sem=hs.at[i], recv_sem=hr.at[i], device_id=dev, device_id_type=MESH
        )
        for i, (s, d, dev) in enumerate(halo)
    ]
    for c in halo:
        c.start()
        pending.append(c.wait_send)

    is_up, is_dn = g < NG - 1, g > 0
    is_right, is_left = b < NB - 1, b > 0
    l_jx.wait()
    l_jy.wait()
    lane = iota((8, CY + 128), 1)
    sub = iota((8, CY + 128), 0)
    outside = ((lane >= CY) & (lane < CY + 64) & jnp.logical_not(is_right)) | (
        (lane >= CY + 64) & jnp.logical_not(is_left)
    )
    inside = jnp.where(outside, 0.0, TIME_STEP).astype(F32)
    ax = [[-0.5 * jx[u, v] for v in range(NV)] for u in range(NV)]
    ay = [[-0.5 * jy[u, v] for v in range(NV)] for u in range(NV)]

    def advance(cur, up, dn, rt, lt, start, scale):
        dx = [p - m for p, m in zip(up, dn)]
        dy = [p - m for p, m in zip(rt, lt)]
        out = []
        for u in range(NV):
            res = DAMPING * ((up[u] + dn[u]) + (rt[u] + lt[u])) - 4.0 * DAMPING * cur[u]
            for v in range(NV):
                res = res + (ax[u][v] * dx[v] + ay[u][v] * dy[v])
            out.append(start[u] + scale * res)
        return out

    def step(cur, prev, nxt, start, scale):
        up = [pltpu.roll(jnp.where(sub == 0, n, q), 7, 0) for n, q in zip(nxt, cur)]
        dn = [pltpu.roll(jnp.where(sub == 7, p, q), 1, 0) for p, q in zip(prev, cur)]
        rt = [pltpu.roll(q, CY + 127, 1) for q in cur]
        lt = [pltpu.roll(q, 1, 1) for q in cur]
        return advance(cur, up, dn, rt, lt, start, scale)

    def rows_at(ref, i):
        r = pl.multiple_of(i * 8, 8)
        return [ref[v, pl.ds(r, 8), :] for v in range(NV)]

    def stage(src, dst, rate, last):
        def tile_at(i):
            row_ok = jnp.where(i == 0, is_dn, jnp.where(i == 17, is_up, True))
            scale = jnp.where(row_ok, rate, 0.0).astype(F32) * inside
            prev, nxt = rows_at(src, jnp.maximum(i - 1, 0)), rows_at(src, jnp.minimum(i + 1, 17))
            new = step(rows_at(src, i), prev, nxt, rows_at(force_q, i), scale)
            for u in range(NV):
                if last:
                    qout[u, pl.ds(pl.multiple_of(i * 8 - 8, 8), 8), :] = new[u][:, 0:CY]
                else:
                    dst[u, pl.ds(pl.multiple_of(i * 8, 8), 8), :] = new[u]

        width = 8 if last else 9

        def body(p, _):
            for t in range(width):
                tile_at(width * p + t + (1 if last else 0))
            return 0

        lax.fori_loop(0, 2, body, 0)

    stage(force_q, qa, RATES[0], False)
    stage(qa, qb, RATES[1], False)
    stage(qb, qa, RATES[2], False)
    stage(qa, None, RATES[3], True)

    for c in halo:
        c.wait_recv()
    zero = jnp.zeros((8, CY + 128), F32)
    zero128 = jnp.zeros((8, 128), F32)

    def wide(x, ok):
        return jnp.concatenate([jnp.where(ok, x, 0.0), zero128], axis=1)

    start = [
        [wide(land_above[v], is_dn) for v in range(NV)],
        [zero] * NV,
        [zero] * NV,
        [wide(land_below[v], is_up) for v in range(NV)],
    ]
    for t in (0, 3):
        for v in range(NV):
            rows0[v, 8 * t : 8 * t + 8, :] = start[t][v]
    nothing = [zero] * NV
    for i, rate in enumerate(RATES):
        src, dst = ((rows0, rows1), (rows1, rows2), (rows2, rows1), (rows1, None))[i]
        for t in (1, 2) if dst is None else range(4):
            def at(k):
                if i == 0 and k in (1, 2):
                    return nothing
                return [src[v, 8 * k : 8 * k + 8, :] for v in range(NV)]

            first = [rows0[v, 8 * t : 8 * t + 8, :] for v in range(NV)] if t in (0, 3) else nothing
            scale = rate * inside
            if t in (0, 3):
                scale = jnp.where(is_dn if t == 0 else is_up, scale, 0.0)
            new = step(at(t), at(t - 1) if t in (1, 3) else nothing, at(t + 1) if t in (0, 2) else nothing, first, scale)
            for u in range(NV):
                if dst is None:
                    r = 0 if t == 1 else CX - 8
                    qout[u, r : r + 8, :] += new[u][:, 0:CY]
                else:
                    dst[u, 8 * t : 8 * t + 8, :] = new[u]

    def sides(right, left, ok):
        from_right = (iota(right.shape, 1) & 7) < 4
        return jnp.where(from_right, jnp.where(is_right & ok, right, 0.0), jnp.where(is_left & ok, left, 0.0))

    mid = sides(land_right[...], land_left[...], True)
    mid = jnp.concatenate([mid, pltpu.roll(mid, 64, 1)], axis=0)
    below = sides(land_corner[0], land_corner[1], is_up)
    above = pltpu.roll(sides(land_corner[2], land_corner[3], is_dn), 64, 1)
    ends = jnp.concatenate([below, jnp.zeros((112, 128), F32), above], axis=0)
    strips = pltpu.roll(jnp.concatenate([mid.T, ends.T], axis=1), 4, 0)
    sub2 = iota((8, 256), 0)
    lane2 = iota((8, 256), 1)
    out_rows = ((lane2 >= 128) & (lane2 < 192) & jnp.logical_not(is_up)) | ((lane2 >= 192) & jnp.logical_not(is_dn))
    inside2 = jnp.where(out_rows, 0.0, TIME_STEP).astype(F32)
    done = []
    for near_side in (True, False):
        start = []
        for v in range(NV):
            x = strips[8 * v : 8 * v + 8]
            start.append(jnp.where((sub2 < 4) == near_side, x, 0.0))
        cur = start
        for rate in RATES:
            up = [pltpu.roll(q, 255, 1) for q in cur]
            dn = [pltpu.roll(q, 1, 1) for q in cur]
            rt = [jnp.where(sub2 == 7, 0.0, pltpu.roll(q, 7, 0)) for q in cur]
            lt = [jnp.where(sub2 == 0, 0.0, pltpu.roll(q, 1, 0)) for q in cur]
            cur = advance(cur, up, dn, rt, lt, start, rate * inside2)
        done.append([q[:, 0:128] for q in cur])
    sub1 = iota((8, 128), 0)
    joined = [jnp.where(sub1 < 4, far, near) for near, far in zip(*done)]
    joined = jnp.concatenate(joined + [jnp.zeros((128 - 8 * NV, 128), F32)], axis=0).T
    lane1 = iota((128, 128), 1)

    def add_columns(v):
        x = pltpu.roll(joined, (124 - 8 * v) % 128, 1)
        qout[v, :, 0:128] += jnp.where(lane1 < 4, x, 0.0)
        qout[v, :, 128:256] += jnp.where(lane1 >= 124, x, 0.0)

    add_columns(NV - 1)

    pres = qout[4]
    pres = jnp.concatenate([pres[:, 0:128].T, pres[:, 128:256].T], axis=1)
    ph, plow = split(pres)
    pres2 = jnp.concatenate([ph, plow], axis=0)
    row16 = iota((16, 128), 0)

    def gather(o, cols):
        h = dot(pres2, cols, NN)
        h = h[0:128] + h[128:256]
        n16 = norms[o]
        forces = []
        for j in range(SEND):
            mask = iota((128, 128), 0) == cellv[o, SEND + j : SEND + j + 1, :]
            p = jnp.sum(jnp.where(mask, h[:, 128 * j : 128 * (j + 1)], 0.0), axis=0, keepdims=True)
            forces.append(jnp.where((row16 & 3) == j, n16 * p, 0.0).astype(BF16))
        return jnp.concatenate(forces, axis=1)

    def gather_four(q, _):
        for first in (0, 2):
            forces = [gather(4 * q + first + i, rall[q, :, 512 * (first + i) : 512 * (first + i + 1)]) for i in range(2)]
            weights = [rbf[4 * q + first + i].reshape(SEND * 128, 128) for i in range(2)]
            both = dot(jnp.concatenate(forces, axis=0), jnp.concatenate(weights, axis=1), NN)
            load_out[4 * q + first] = both[0:16, 0:128]
            load_out[4 * q + first + 1] = both[16:32, 128:256]
        return 0

    for q in (1, 3, 2, 0):
        lax.fori_loop(q, q + 1, gather_four, 0)
        blk_send(lambda o: load_out.at[o], land_load, 3, [o for o in reversed(range(4 * q, 4 * q + 4)) if o != ME])
    land_load[ME] = load_out[ME]
    for v in range(NV - 1):
        add_columns(v)
    flow_out = pltpu.make_async_copy(qout, flow_o, osem.at[0])
    flow_out.start()
    pending.append(flow_out.wait)

    l_secv.wait()
    zero8 = jnp.zeros((8, 128), F32)

    def gram_row(i, _):
        for c in range(3):
            x = secv[:, c, pl.ds(i, 1), :].reshape(COLS, 128)
            x = jnp.where((i >= off) & (i < off + OWN), x, 0.0)
            hi, lo = split(jnp.concatenate([x, zero8], axis=0))
            at = pl.multiple_of((c * WIN + i) * 128, 128)
            zmat[0:32, pl.ds(at, 128)] = hi
            zmat[32:64, pl.ds(at, 128)] = lo
        return 0

    lax.fori_loop(0, WIN, gram_row, 0)
    zz = zmat[...]
    top = dot(zz, zz[0:32], NT)
    low = dot(zz, zz[32:64], NT)
    gram = top[0:32] + top[32:64] + low[0:32] + low[32:64]
    gsend[...] = jnp.zeros(gsend.shape, F32)
    gsend[:, 0:32] = gram
    land_gg[g] = gsend[...]
    grp_send(lambda d: gsend, land_gg, 0)

    row = iota((COLS, 128), 0)
    lane = iota((COLS, 128), 1)
    wrow = iota((48, 128), 0) & 15
    mine = (wrow >= off) & (wrow < off + OWN)
    d_in = jnp.where(mine, disp[:, pl.ds(a, WIN), :].reshape(48, 128), 0.0)
    rhs_in = jnp.sum(secv[...].reshape(COLS, 48, 128) * d_in[None], axis=1)
    diag = lane == row + 32

    blk_recv(lambda o: req.at[peer(o)], land_req, 0, [FAR])
    asked_t = land_req[...].reshape(NB * 16, 128).T[0:1, :]
    rr, kk = iota((48, NB * 16), 0), iota((48, NB * 16), 1)
    w = rr & 15
    same_c = (lax.shift_right_logical(kk, 2) & 3) == lax.shift_right_logical(rr, 4)
    for p in range(NG):
        first = (p * OWN) // 8 * 8
        skip = p * OWN - first
        ok = same_c & (w >= skip) & (w < skip + OWN)
        oht[48 * p : 48 * (p + 1), :] = jnp.where(ok & (asked_t == (w + first).astype(F32)), 1.0, 0.0).astype(BF16)

    blk_recv(lambda o: load_out.at[o], land_load, 3)
    got = land_load[...].reshape(NB * 16, 128)
    hi, lo = split(got)
    sums = dot(oht[...], jnp.concatenate([hi, lo], axis=1), NN)
    part[...] = (sums[:, 0:128] + sums[:, 128:256]).reshape(NG, 48, 128)
    land_part[g] = part[g]
    grp_send(lambda d: part.at[d], land_part, 1)
    l_flex.wait()

    def project(i, _):
        at = pl.multiple_of(128 * i, 128)
        hi, lo = split(flex[i])
        flexhl[pl.ds(at, 128), 0:128] = hi
        flexhl[pl.ds(at, 128), 128:256] = lo
        vh, vl = split(jnp.concatenate([secv[:, c, pl.ds(i, 1), :].reshape(COLS, 128) for c in range(3)], axis=0))
        u = dot(jnp.concatenate([vh, vl], axis=0), hi, NN)
        u = u[0:72] + u[72:144] + dot(vh, lo, NN)
        for c in range(3):
            uwin[:, c, pl.ds(i, 1), :] = u[COLS * c : COLS * (c + 1)].reshape(COLS, 1, 128)
        return 0

    lax.fori_loop(0, WIN, project, 0)
    grp_recv(lambda d: gsend, land_gg, 0)
    gsum[...] = jnp.sum(land_gg[...], axis=0)
    land_gb[ME] = gsum[...]
    blk_send(lambda o: gsum, land_gb, 2)
    grp_recv(lambda d: part.at[d], land_part, 1)
    tile_loads = jnp.sum(land_part[...], axis=0)

    prod = jnp.sum(uwin[...].reshape(COLS, 48, 128) * tile_loads[None], axis=1) - rhs_in
    rhs = jnp.sum(prod, axis=1, keepdims=True)
    rhs = jnp.sum(jnp.where(diag, rhs, 0.0), axis=0, keepdims=True)
    rmsg[...] = jnp.broadcast_to(rhs, (8, 128))
    land_rg[g] = rmsg[...]
    grp_send(lambda d: rmsg, land_rg, 2)
    hi, lo = split(tile_loads)
    lhs = jnp.concatenate(
        [jnp.concatenate([hi, hi], axis=1), jnp.concatenate([lo, jnp.zeros_like(lo)], axis=1)], axis=0
    )
    tilde = jnp.zeros((48, 128), F32)
    for u in range(WIN // 2):
        o = dot(lhs, flexhl[256 * u : 256 * (u + 1), :], NT)
        o = o[0:48] + o[48:96]
        tilde = jnp.where(wrow == 2 * u, o[:, 0:128], tilde)
        tilde = jnp.where(wrow == 2 * u + 1, o[:, 128:256], tilde)
    tmsg[...] = jnp.where(mine, tilde, 0.0)
    land_t[g] = tmsg[...]
    grp_send(lambda d: tmsg, land_t, 3)
    grp_recv(lambda d: rmsg, land_rg, 2)
    rsend[...] = jnp.sum(land_rg[...], axis=0)
    land_r[ME] = rsend[...]
    blk_send(lambda o: rsend, land_r, 4)
    l_secw.wait()
    blk_recv(lambda o: gsum, land_gb, 2)
    gram = jnp.sum(land_gb[...], axis=0)[0:COLS]
    row = iota((COLS, 128), 0)
    lane = iota((COLS, 128), 1)
    m = jnp.where(lane < COLS, gram, jnp.where(lane == row + 32, 1.0, 0.0))
    fac = jnp.zeros((COLS, 128), F32)
    for k in range(COLS):
        pivot = lax.rsqrt(jnp.broadcast_to(m[k : k + 1, k : k + 1], (1, 128)))
        r = m[k : k + 1, :] * pivot
        col = jnp.broadcast_to(m[:, k : k + 1], (COLS, 128)) * pivot
        fac = jnp.where(row == k, r, fac)
        m = m - jnp.where(row > k, col * r, 0.0)
    linv[...] = jnp.where((lane >= 32) & (lane < 32 + COLS), fac, 0.0)
    grp_recv(lambda d: tmsg, land_t, 3)
    blk_recv(lambda o: rsend, land_r, 4)
    rhs = jnp.sum(land_r[...], axis=0)[0:1]

    li = linv[...]
    y = jnp.sum(li * rhs, axis=1, keepdims=True)
    x = jnp.sum(li * y, axis=0, keepdims=True)
    x = -jnp.sum(jnp.where(diag, x, 0.0), axis=1, keepdims=True)
    coef[...] = jnp.broadcast_to(x, (COLS, 128))

    def update(p, _):
        for c in range(3):
            even, odd = land_t[2 * p, 16 * c : 16 * c + 16, :], land_t[2 * p + 1, 16 * c : 16 * c + 16, :]
            for q, t in enumerate((even[0:8], even[8:16] + odd[0:8], odd[8:16])):
                at = pl.multiple_of(24 * p + 8 * q, 8)
                for k in range(COLS):
                    t = t + coef[k : k + 1, :] * secw[k, c, pl.ds(at, 8), :]
                dout[c, pl.ds(at, 8), :] = t
        return 0

    lax.fori_loop(0, NG // 2, update, 0)
    disp_out = pltpu.make_async_copy(dout, disp_o, osem.at[1])
    disp_out.start()
    pending.append(disp_out.wait)

    finish()


def deliver(flow, disp, flow_out, disp_out, sems):
    copies = [pltpu.make_async_copy(flow, flow_out, sems.at[0]), pltpu.make_async_copy(disp, disp_out, sems.at[1])]
    for c in copies:
        c.start()
    for c in copies:
        c.wait()


def stay(x):
    return pltpu.with_memory_space_constraint(x, pltpu.HBM)


def on_device(flow_state, jx, jy, slot_tile, slot_cells, slot_normal, slot_rbf, disp_in, flex, secv, secw):
    hbm = pl.BlockSpec(memory_space=pl.ANY)
    vm, dma = pltpu.VMEM, pltpu.SemaphoreType.DMA
    state = (NV, CX + 16, CY + 128)
    scratch = [
        pltpu.SMEM((NV, NV), F32), pltpu.SMEM((NV, NV), F32),
        vm((1, 64), jnp.int32), vm((64, 128), jnp.int32), vm((3, 64, 128), F32), vm((NB, SEND, 128, 128), BF16),
        vm((3, ST, 128), F32), vm((WIN, 128, 128), F32), vm((COLS, 3, WIN, 128), F32), vm((COLS, 3, ST, 128), F32),
        vm(state, F32), vm(state, F32), vm(state, F32), vm((NV, CX, CY), F32),
        vm((NV, 32, CY + 128), F32), vm((NV, 32, CY + 128), F32), vm((NV, 32, CY + 128), F32),
        vm((NB, 16, 128), F32), vm((NB, 16, 128), F32), vm((NB, 16, 128), BF16), vm((NB, 16, 128), BF16),
        vm((384, 128), BF16),
        vm((NB, 8, 128), jnp.int32), vm((4, 256, 2048), BF16), vm((4, 256, 2048), F8),
        vm((384, 2048), BF16), vm((384, 2048), F8), vm((384, 256), F32), vm((384, 128), BF16),
        vm((64, 128), F32),
        vm((NV, 8, CY), F32), vm((NV, 8, CY), F32), vm((64, 128), F32), vm((64, 128), F32), vm((4, 8, 128), F32),
        vm((256, 128), F32), vm((NB, 16, 128), F32), vm((NB, 16, 128), F32), vm((NB, 16, 128), F32), vm((384, 256), BF16),
        vm((NG, 48, 128), F32), vm((NG, 48, 128), F32),
        vm((WIN * 128, 256), BF16), vm((COLS, 3, WIN, 128), F32), vm((64, 48 * 128), BF16),
        vm((32, 128), F32), vm((NG, 32, 128), F32), vm((32, 128), F32), vm((NB, 32, 128), F32), vm((COLS, 128), F32),
        vm((8, 128), F32), vm((NG, 8, 128), F32), vm((48, 128), F32), vm((NG, 48, 128), F32),
        vm((8, 128), F32), vm((NB, 8, 128), F32), vm((COLS, 128), F32), vm((3, ST, 128), F32),
        dma((10,)), dma((NB,)), dma((4,)),
        dma((5, NB)), dma((5, NB)), dma((4, NG)), dma((4, NG)), dma((8,)), dma((8,)),
    ]
    flow_out, disp_out = pl.pallas_call(
        kernel,
        out_shape=(
            vm((NV, CX, CY), F32),
            vm((3, ST, 128), F32),
        ),
        in_specs=[hbm] * 11,
        out_specs=(hbm, hbm),
        scratch_shapes=scratch,
        compiler_params=pltpu.CompilerParams(
            collective_id=0, has_side_effects=True, vmem_limit_bytes=48 * 1024 * 1024
        ),
    )(*[
        stay(x) for x in (
            flow_state, jx, jy, slot_tile.reshape(1, -1), slot_cells, jnp.transpose(slot_normal, (1, 0, 2)), slot_rbf,
            jnp.transpose(disp_in, (1, 0, 2)), flex, jnp.transpose(secv, (0, 2, 1, 3)), jnp.transpose(secw, (0, 2, 1, 3)),
        )
    ])
    flow_out, disp_out = pl.pallas_call(
        deliver,
        out_shape=(jax.ShapeDtypeStruct(flow_out.shape, F32), jax.ShapeDtypeStruct(disp_out.shape, F32)),
        in_specs=[hbm, hbm],
        out_specs=(hbm, hbm),
        scratch_shapes=[dma((2,))],
        compiler_params=pltpu.CompilerParams(vmem_limit_bytes=1024 * 1024),
    )(flow_out, disp_out)
    return flow_out, jnp.transpose(disp_out, (1, 0, 2))


def solution(mesh):
    placed = (
        P(None, "grp", "blk"), P(), P(),
        P(("grp", "blk")), P(("grp", "blk"), None),
        P(("grp", "blk"), None, None), P(("grp", "blk"), None, None),
        P("blk", None, None), P("blk", None, None),
        P(None, "blk", None, None), P(None, "blk", None, None),
    )
    return jax.shard_map(
        on_device, mesh=mesh, in_specs=placed,
        out_specs=(P(None, "grp", "blk"), P("blk", None, None)), check_vma=False,
    )
```

profile of v0, /device:TPU:0, one launch (start us, length us, event | category | flops | bytes accessed | tf_op | source)
XLA Modules:
  0.0 53.2 jit_solution(10622568480633636743)
XLA Ops:
  0.6 51.7 %shard_map.122 = (f32[5,128,256]{2,1,0:T(8,128)S(1)}, f32[3,96,128]{2,1,0:T(8,128)S(1)}) custom-call(f32[5,128,256]{2,1,0:T(8,128)} %flow_h.1, f32[5,5]{1,0:T(8,128)} %jx_h.1, f32[5,5]{1,0:T(8,128)} %jy_h.1, s32[1,64]{1,0:T(1,128)} %bitcast.10, s32[64,128]{1,0:T(8,128)} %cells_h.1, f32[3,64,128]{2,1,0:T(8,128)} %bitcast.9, bf16[64,128,128]{2,1,0:T(8,128)(2,1)} %rbf_h.1, ...), custom_call_target="tpu_custom_call" | custom-call | tf_op jit(solution)/shard_map/pallas_call | solution.py:656
  52.3 0.9 %shard_map.123 = (f32[5,128,256]{2,1,0:T(8,128)}, f32[3,96,128]{2,1,0:T(8,128)}) custom-call(f32[5,128,256]{2,1,0:T(8,128)S(1)} %get-tuple-element.6.flow, f32[3,96,128]{2,1,0:T(8,128)S(1)} %get-tuple-element.7.disp), custom_call_target="tpu_custom_call" | custom-call | tf_op jit(solution)/shard_map/pallas_call | solution.py:674
where the time goes:
time: 53.8 us; the launch traced here: 53.2 us
  Pallas kernels  52.6 us (98%)
  between operations  0.64 us (1%)
    pallas_call x1, Pallas kernels, on_device(): pl.pallas_call(kernel, out_shape=(vm((NV, CX, CY), F32), vm((3, ST, 128),...  51.7 us

commit v1 on v0

--- a/solution.py
+++ b/solution.py
@@ -474,11 +474,6 @@
         lax.fori_loop(q, q + 1, gather_four, 0)
         blk_send(lambda o: load_out.at[o], land_load, 3, [o for o in reversed(range(4 * q, 4 * q + 4)) if o != ME])
     land_load[ME] = load_out[ME]
-    for v in range(NV - 1):
-        add_columns(v)
-    flow_out = pltpu.make_async_copy(qout, flow_o, osem.at[0])
-    flow_out.start()
-    pending.append(flow_out.wait)
 
     l_secv.wait()
     zero8 = jnp.zeros((8, 128), F32)
@@ -507,8 +502,6 @@
     lane = iota((COLS, 128), 1)
     wrow = iota((48, 128), 0) & 15
     mine = (wrow >= off) & (wrow < off + OWN)
-    d_in = jnp.where(mine, disp[:, pl.ds(a, WIN), :].reshape(48, 128), 0.0)
-    rhs_in = jnp.sum(secv[...].reshape(COLS, 48, 128) * d_in[None], axis=1)
     diag = lane == row + 32
 
     blk_recv(lambda o: req.at[peer(o)], land_req, 0, [FAR])
@@ -529,6 +522,13 @@
     part[...] = (sums[:, 0:128] + sums[:, 128:256]).reshape(NG, 48, 128)
     land_part[g] = part[g]
     grp_send(lambda d: part.at[d], land_part, 1)
+    for v in range(NV - 1):
+        add_columns(v)
+    flow_out = pltpu.make_async_copy(qout, flow_o, osem.at[0])
+    flow_out.start()
+    pending.append(flow_out.wait)
+    d_in = jnp.where(mine, disp[:, pl.ds(a, WIN), :].reshape(48, 128), 0.0)
+    rhs_in = jnp.sum(secv[...].reshape(COLS, 48, 128) * d_in[None], axis=1)
     l_flex.wait()
 
     def project(i, _):

time: 53.8 us -> 53.8 us (level)
  no operation moved by 1% of the time
where the time goes in v1:
time: 53.8 us; the launch traced here: 53.4 us
  Pallas kernels  52.8 us (98%)
  between operations  0.64 us (1%)
    pallas_call x1, Pallas kernels, on_device(): pl.pallas_call(kernel, out_shape=(vm((NV, CX, CY), F32), vm((3, ST, 128),...  51.9 us

profile of v1, /device:TPU:0, one launch (start us, length us, event | category | flops | bytes accessed | tf_op | source)
XLA Modules:
  0.0 53.4 jit_solution(6411307640697292114)
XLA Ops:
  0.6 51.9 %shard_map.122 = (f32[5,128,256]{2,1,0:T(8,128)S(1)}, f32[3,96,128]{2,1,0:T(8,128)S(1)}) custom-call(f32[5,128,256]{2,1,0:T(8,128)} %flow_h.1, f32[5,5]{1,0:T(8,128)} %jx_h.1, f32[5,5]{1,0:T(8,128)} %jy_h.1, s32[1,64]{1,0:T(1,128)} %bitcast.10, s32[64,128]{1,0:T(8,128)} %cells_h.1, f32[3,64,128]{2,1,0:T(8,128)} %bitcast.9, bf16[64,128,128]{2,1,0:T(8,128)(2,1)} %rbf_h.1, ...), custom_call_target="tpu_custom_call" | custom-call | tf_op jit(solution)/shard_map/pallas_call | solution.py:656
  52.5 0.9 %shard_map.123 = (f32[5,128,256]{2,1,0:T(8,128)}, f32[3,96,128]{2,1,0:T(8,128)}) custom-call(f32[5,128,256]{2,1,0:T(8,128)S(1)} %get-tuple-element.6.flow, f32[3,96,128]{2,1,0:T(8,128)S(1)} %get-tuple-element.7.disp), custom_call_target="tpu_custom_call" | custom-call | tf_op jit(solution)/shard_map/pallas_call | solution.py:674
